TPU v7x, 32 devices: a whole 2x2x4 slice. The times are simulated.
32 devices in a mesh: gy: 4 (over z), gx: 8 (over y, x, core).
Axes of the slice: x: 2, y: 2, z: 4, core: 2. Of those that a mesh axis runs over, the one named last changes fastest.
Arguments:
- saved_thickness: bfloat16 [2, 256, 2048], P(None, 'gy', 'gx'), may hold values from 0.5 to 2
- saved_velocity: bfloat16 [2, 2, 256, 2048], P(None, None, 'gy', 'gx'), may hold values from -4 to 4
- surface_slope: bfloat16 [2, 256, 2048], P(None, 'gy', 'gx'), may hold values from -3 to 3
- basal_beta: float32 [256, 2048], P('gy', 'gx'), may hold values from 0.2 to 5
- cell_mask: int32 [256, 2048], P('gy', 'gx'), may hold values from 0 to 2
- upwind_flags: int32 [256, 2048], P('gy', 'gx'), may hold values from 0 to 3
- observed_velocity: bfloat16 [2, 2, 256, 2048], P(None, None, 'gy', 'gx'), may hold values from -60 to 60
- thickness_adjoint: float32 [256, 2048], P('gy', 'gx'), may hold values from -6 to 6
Outputs:
- beta_gradient: float32 [256, 2048], P('gy', 'gx')
- thickness_gradient: float32 [256, 2048], P('gy', 'gx')
- misfit: float32 [], replicated
All inputs are finite; a program needn't handle non-finite values.
Results may differ from a plain program's by a relative error of at most 0.0003.
Values sent between devices are 32-bit elements; how exact they have to be, the bound alone decides.
A program may use at most 64 MiB of HBM per device.

v0:
```python
import jax
import jax.numpy as jnp
from jax import lax
from jax.sharding import PartitionSpec as P

SWEEPS = 3


RELAXATION = 0.8
TIME_STEP = 0.1
EPSILON = 1e-06
DEEP_WIDTH = 8
OFFSETS = ((0, 1), (2, 1), (1, 0), (1, 2))


def padded_2(block, sides, width):
    for axis, dim in sides:
        count = lax.axis_size(axis)
        forward = [(i, i + 1) for i in range(count - 1)]
        backward = [(target, source) for source, target in forward]
        low = lax.ppermute(
            lax.slice_in_dim(block, block.shape[dim] - width, None, axis=dim), axis, forward
        )
        high = lax.ppermute(lax.slice_in_dim(block, 0, width, axis=dim), axis, backward)
        block = jnp.concatenate([low, block, high], axis=dim)
    return block


def shifted(padded, row_offset, col_offset):
    row_count = padded.shape[-2] - 2
    col_count = padded.shape[-1] - 2
    return padded[..., row_offset : row_offset + row_count, col_offset : col_offset + col_count]


def pad_one(values):
    widths = [(0, 0)] * (values.ndim - 2) + [(1, 1), (1, 1)]
    return jnp.pad(values, widths)


def sweep_core(velocity_pad, thick_pad, cover_pad, friction, forcing):
    center = shifted(velocity_pad, 1, 1)
    thick_mid = shifted(thick_pad, 1, 1)
    cover_mid = shifted(cover_pad, 1, 1)
    flux_sum = jnp.zeros_like(center)
    coupling_sum = jnp.zeros_like(thick_mid)
    for row_offset, col_offset in OFFSETS:
        difference = shifted(velocity_pad, row_offset, col_offset) - center
        strain = jnp.sum(difference * difference, axis=0)
        coupling = (
            0.5
            * (thick_mid + shifted(thick_pad, row_offset, col_offset))
            * cover_mid
            * shifted(cover_pad, row_offset, col_offset)
            * jnp.power(1.0 + strain, -1.0 / 3.0)
        )
        flux_sum = flux_sum + coupling * difference
        coupling_sum = coupling_sum + coupling
    residual = forcing - friction * center + flux_sum
    return cover_mid * (center + RELAXATION * residual / (1.0 + friction + coupling_sum))


def transport_core(thick_pad, velocity_pad, cover_pad, donor_east_pad, donor_south_pad):
    east_cover = cover_pad[1:-1, :-1] * cover_pad[1:-1, 1:]
    speed_east = 0.5 * (velocity_pad[0, 1:-1, :-1] + velocity_pad[0, 1:-1, 1:])
    donor_east = donor_east_pad[1:-1, :-1]
    flux_east = (
        speed_east
        * east_cover
        * (donor_east * thick_pad[1:-1, :-1] + (1.0 - donor_east) * thick_pad[1:-1, 1:])
    )
    south_cover = cover_pad[:-1, 1:-1] * cover_pad[1:, 1:-1]
    speed_south = 0.5 * (velocity_pad[1, :-1, 1:-1] + velocity_pad[1, 1:, 1:-1])
    donor_south = donor_south_pad[:-1, 1:-1]
    flux_south = (
        speed_south
        * south_cover
        * (donor_south * thick_pad[:-1, 1:-1] + (1.0 - donor_south) * thick_pad[1:, 1:-1])
    )
    diverge = flux_east[:, 1:] - flux_east[:, :-1] + flux_south[1:, :] - flux_south[:-1, :]
    return cover_pad[1:-1, 1:-1] * (thick_pad[1:-1, 1:-1] - TIME_STEP * diverge)


def deep_step(
    thick_field,
    friction_field,
    start_field,
    slope_deep,
    cover_pad_deep,
    east_pad_deep,
    south_pad_deep,
):
    forcing = thick_field * slope_deep
    thick_pad = pad_one(thick_field)
    velocity = start_field
    sweep_step = jax.checkpoint(sweep_core)
    for sweep_index in range(SWEEPS):
        velocity = sweep_step(pad_one(velocity), thick_pad, cover_pad_deep, friction_field, forcing)
    thick_next = jax.checkpoint(transport_core)(
        thick_pad, pad_one(velocity), cover_pad_deep, east_pad_deep, south_pad_deep
    )
    return (velocity, thick_next)


def on_device(
    saved_thickness,
    saved_velocity,
    surface_slope,
    basal_beta,
    cell_mask,
    upwind_flags,
    observed_velocity,
    thickness_adjoint,
):
    cover = (cell_mask > 0).astype(jnp.float32)
    grounded = (cell_mask == 2).astype(jnp.float32)
    friction = basal_beta * grounded
    slope_field = surface_slope.astype(jnp.float32)
    donor_east = (upwind_flags % 2).astype(jnp.float32)
    donor_south = (upwind_flags // 2).astype(jnp.float32)
    inner = DEEP_WIDTH
    deep_statics = jnp.concatenate(
        [jnp.stack([cover, donor_east, donor_south, friction, grounded]), slope_field], axis=0
    )
    deep_fixed = padded_2(deep_statics, (("gy", 1), ("gx", 2)), 8)
    cover_pad_deep = pad_one(deep_fixed[0])
    east_pad_deep = pad_one(deep_fixed[1])
    south_pad_deep = pad_one(deep_fixed[2])
    friction_deep = deep_fixed[3]
    grounded_deep = deep_fixed[4]
    slope_deep = deep_fixed[5:7]
    cell_count = (
        saved_thickness.shape[1]
        * saved_thickness.shape[2]
        * lax.axis_size("gy")
        * lax.axis_size("gx")
    )
    cotangent = thickness_adjoint
    beta_gradient = jnp.zeros_like(basal_beta)
    misfit = jnp.zeros((), jnp.float32)
    for step_index in reversed(range(saved_thickness.shape[0])):
        thickness = saved_thickness[step_index].astype(jnp.float32)
        velocity = saved_velocity[step_index].astype(jnp.float32)
        observed = observed_velocity[step_index].astype(jnp.float32)
        step_joined = padded_2(
            jnp.concatenate([velocity, thickness[None], cotangent[None], observed], axis=0),
            (("gy", 1), ("gx", 2)),
            8,
        )
        start_deep = step_joined[0:2]
        cotangent_deep = step_joined[3]
        observed_deep = step_joined[4:6]

        def advance(thick_field, friction_field):
            return deep_step(
                thick_field,
                friction_field,
                start_deep,
                slope_deep,
                cover_pad_deep,
                east_pad_deep,
                south_pad_deep,
            )

        (velocity_deep, unused_next), deep_pullback = jax.vjp(
            advance, step_joined[2], friction_deep
        )
        velocity = velocity_deep[:, inner:-inner, inner:-inner]
        difference = velocity - observed
        misfit_field = grounded * difference
        local_misfit = 0.5 * jnp.sum(misfit_field * difference)
        local_scale = jnp.sum(grounded * jnp.sum(observed * observed, axis=0))
        misfit_total, scale_total = lax.psum((local_misfit, local_scale), ("gy", "gx"))
        misfit_scale = scale_total / cell_count + EPSILON
        misfit = misfit + misfit_total / cell_count / misfit_scale
        misfit_seed = grounded_deep * (velocity_deep - observed_deep) / misfit_scale
        thick_grad, friction_grad = deep_pullback((misfit_seed, cotangent_deep))
        beta_gradient = beta_gradient + grounded * friction_grad[inner:-inner, inner:-inner]
        cotangent = thick_grad[inner:-inner, inner:-inner]
    return (beta_gradient, cotangent, misfit)


def solution(mesh):
    in_specs = (
        P(None, "gy", "gx"),
        P(None, None, "gy", "gx"),
        P(None, "gy", "gx"),
        P("gy", "gx"),
        P("gy", "gx"),
        P("gy", "gx"),
        P(None, None, "gy", "gx"),
        P("gy", "gx"),
    )
    out_specs = (P("gy", "gx"), P("gy", "gx"), P())
    return jax.shard_map(
        on_device, mesh=mesh, in_specs=in_specs, out_specs=out_specs, check_vma=False
    )
```

profile of v0, /device:TPU:0, one launch (start us, length us, event | category | flops | bytes accessed | tf_op | source)
XLA Modules:
  0.0 192.9 jit_solution(8931833436882227988)
XLA Ops:
  0.6 1.5 fusion.56
  4.8 5.1 %collective-permute-start = (f32[7,8,256]{2,1,0:T(8,128)S(1)}, f32[7,8,256]{2,1,0:T(8,128)S(1)}, u32[]{:S(2)}, u32[]{:S(2)}) collective-permute-start(f32[7,8,256]{2,1,0:T(8,128)S(1)} %get-tuple-element.401), channel_id=1, source_target_pairs={{0,8},{8,16},{16,24},{1,9},{9,17},{17,25},{2,10},{10,18},{18,26},{... | collective-permute-start | bytes 172040 | tf_op jit(solution)/shard_map/ppermute | solution.py:21
  11.6 3.5 %collective-permute-start.4 = (f32[6,8,256]{2,1,0:T(8,128)S(1)}, f32[6,8,256]{2,1,0:T(8,128)S(1)}, u32[]{:S(2)}, u32[]{:S(2)}) collective-permute-start(f32[6,8,256]{2,1,0:T(8,128)S(1)} %get-tuple-element.405), channel_id=1, source_target_pairs={{0,8},{8,16},{16,24},{1,9},{9,17},{17,25},{2,10},{10,18},{18,26},{... | collective-permute-start | bytes 147464 | tf_op jit(solution)/shard_map/ppermute | solution.py:21
  15.1 1.3 collective-permute-start.5
  17.1 1.3 collective-permute-start.1
  18.3 43.0 %psum.28 = f32[]{:T(128)} all-reduce(f32[]{:T(128)} %select_reduce_fusion.1), channel_id=1, replica_groups=mesh['gy'=4,'gx'=8] {'gy','gx'}, use_global_device_ids=true, to_apply=%region_14.15 | all-reduce | flops 1 | bytes 8 | tf_op jit(solution)/shard_map/psum | solution.py:172
  62.1 1.3 collective-permute-start.6
  63.5 1.3 collective-permute-start.7
  65.0 5.5 %collective-permute-start.2 = (f32[7,80,8]{2,1,0:T(8,128)S(1)}, f32[7,80,8]{2,1,0:T(8,128)S(1)}, u32[]{:S(2)}, u32[]{:S(2)}) collective-permute-start(f32[7,80,8]{2,1,0:T(8,128)S(1)} %get-tuple-element.391), channel_id=1, source_target_pairs={{0,1},{1,2},{2,3},{3,4},{4,5},{5,6},{6,7},{8,9},{9,10},{10,11},{11... | collective-permute-start | bytes 53768 | tf_op jit(solution)/shard_map/ppermute | solution.py:21
  70.5 1.3 collective-permute-start.3
  72.7 2.5 %collective-permute-done.3 = f32[7,80,8]{2,1,0:T(8,128)S(1)} collective-permute-done((f32[7,80,8]{2,1,0:T(8,128)S(1)}, f32[7,80,8]{2,1,0:T(8,128)S(1)}, u32[]{:S(2)}, u32[]{:S(2)}) %collective-permute-start.3) | collective-permute-done | bytes 17952 | tf_op jit(solution)/shard_map/ppermute | solution.py:24
  82.9 1.4 add_add_fusion.27
  86.9 1.4 add_add_fusion.26
  91.6 1.3 add_add_fusion.25
  93.3 3.4 %collective-permute-start.8 = (f32[6,8,256]{2,1,0:T(8,128)S(1)}, f32[6,8,256]{2,1,0:T(8,128)S(1)}, u32[]{:S(2)}, u32[]{:S(2)}) collective-permute-start(f32[6,8,256]{2,1,0:T(8,128)S(1)} %get-tuple-element.403), channel_id=1, source_target_pairs={{0,8},{8,16},{16,24},{1,9},{9,17},{17,25},{2,10},{10,18},{18,26},{... | collective-permute-start | bytes 147464 | tf_op jit(solution)/shard_map/ppermute | solution.py:21
  96.7 1.3 collective-permute-start.9
  98.4 4.3 %collective-permute-done.9 = f32[6,8,256]{2,1,0:T(8,128)S(1)} collective-permute-done((f32[6,8,256]{2,1,0:T(8,128)S(1)}, f32[6,8,256]{2,1,0:T(8,128)S(1)}, u32[]{:S(2)}, u32[]{:S(2)}) %collective-permute-start.9) | collective-permute-done | bytes 49184 | tf_op jit(solution)/shard_map/ppermute | solution.py:24
  102.8 6.9 %collective-permute-start.10 = (f32[6,80,8]{2,1,0:T(8,128)S(1)}, f32[6,80,8]{2,1,0:T(8,128)S(1)}, u32[]{:S(2)}, u32[]{:S(2)}) collective-permute-start(f32[6,80,8]{2,1,0:T(8,128)S(1)} %get-tuple-element.397), channel_id=1, source_target_pairs={{0,1},{1,2},{2,3},{3,4},{4,5},{5,6},{6,7},{8,9},{9,10},{10,11},{11... | collective-permute-start | bytes 46088 | tf_op jit(solution)/shard_map/ppermute | solution.py:21
  109.7 1.3 collective-permute-start.11
  111.0 2.9 %collective-permute-done.11 = f32[6,80,8]{2,1,0:T(8,128)S(1)} collective-permute-done((f32[6,80,8]{2,1,0:T(8,128)S(1)}, f32[6,80,8]{2,1,0:T(8,128)S(1)}, u32[]{:S(2)}, u32[]{:S(2)}) %collective-permute-start.11) | collective-permute-done | bytes 15392 | tf_op jit(solution)/shard_map/ppermute | solution.py:24
  122.5 45.2 %all-reduce.89 = (f32[]{:T(128)}, f32[]{:T(128)}, f32[]{:T(128)}) all-reduce(f32[]{:T(128)} %select_reduce_fusion, f32[]{:T(128)S(6)} %mul.3032, f32[]{:T(128)S(6)} %mul.3035), channel_id=1, replica_groups=mesh['gy'=4,'gx'=8] {'gy','gx'}, use_global_device_ids=true, to_apply=%region_60.61 | all-reduce | flops 3 | bytes 24 | tf_op jit(solution)/shard_map/psum | solution.py:172
  173.5 1.2 fusion
  178.0 1.7 add_add_fusion.18
  182.3 1.6 add_add_fusion.17
  (217 shorter events, 44.8 us)
Async XLA Ops:
  0.6 1.6 copy-start.38
  4.8 5.1 %copy-start.41 = (bf16[2,2,64,256]{3,2,1,0:T(8,128)(2,1)S(1)}, bf16[2,2,64,256]{3,2,1,0:T(8,128)(2,1)}, u32[]{:S(2)}) copy-start(bf16[2,2,64,256]{3,2,1,0:T(8,128)(2,1)} %param.9) | copy-start | bytes 393220
  4.8 5.1 %copy-start.6 = (bf16[2,2,64,256]{3,2,1,0:T(8,128)(2,1)S(1)}, bf16[2,2,64,256]{3,2,1,0:T(8,128)(2,1)}, u32[]{:S(2)}) copy-start(bf16[2,2,64,256]{3,2,1,0:T(8,128)(2,1)} %param.14) | copy-start | bytes 393220
  4.8 59.9 %collective-permute-start = (f32[7,8,256]{2,1,0:T(8,128)S(1)}, f32[7,8,256]{2,1,0:T(8,128)S(1)}, u32[]{:S(2)}, u32[]{:S(2)}) collective-permute-start(f32[7,8,256]{2,1,0:T(8,128)S(1)} %get-tuple-element.401), channel_id=1, source_target_pairs={{0,8},{8,16},{16,24},{1,9},{9,17},{17,25},{2,10},{10,18},{18,26},{... | collective-permute-start | bytes 172040 | tf_op jit(solution)/shard_map/ppermute | solution.py:21
  11.6 50.3 %collective-permute-start.4 = (f32[6,8,256]{2,1,0:T(8,128)S(1)}, f32[6,8,256]{2,1,0:T(8,128)S(1)}, u32[]{:S(2)}, u32[]{:S(2)}) collective-permute-start(f32[6,8,256]{2,1,0:T(8,128)S(1)} %get-tuple-element.405), channel_id=1, source_target_pairs={{0,8},{8,16},{16,24},{1,9},{9,17},{17,25},{2,10},{10,18},{18,26},{... | collective-permute-start | bytes 147464 | tf_op jit(solution)/shard_map/ppermute | solution.py:21
  15.1 46.9 %collective-permute-start.5 = (f32[6,8,256]{2,1,0:T(8,128)S(1)}, f32[6,8,256]{2,1,0:T(8,128)S(1)}, u32[]{:S(2)}, u32[]{:S(2)}) collective-permute-start(f32[6,8,256]{2,1,0:T(8,128)S(1)} %get-tuple-element.406), channel_id=1, source_target_pairs={{8,0},{16,8},{24,16},{9,1},{17,9},{25,17},{10,2},{18,10},{26,18},{... | collective-permute-start | bytes 147464 | tf_op jit(solution)/shard_map/ppermute | solution.py:24
  17.1 47.7 %collective-permute-start.1 = (f32[7,8,256]{2,1,0:T(8,128)S(1)}, f32[7,8,256]{2,1,0:T(8,128)S(1)}, u32[]{:S(2)}, u32[]{:S(2)}) collective-permute-start(f32[7,8,256]{2,1,0:T(8,128)S(1)} %get-tuple-element.402), channel_id=1, source_target_pairs={{8,0},{16,8},{24,16},{9,1},{17,9},{25,17},{10,2},{18,10},{26,18},{... | collective-permute-start | bytes 172040 | tf_op jit(solution)/shard_map/ppermute | solution.py:24
  62.1 9.7 %collective-permute-start.6 = (f32[6,80,8]{2,1,0:T(8,128)S(1)}, f32[6,80,8]{2,1,0:T(8,128)S(1)}, u32[]{:S(2)}, u32[]{:S(2)}) collective-permute-start(f32[6,80,8]{2,1,0:T(8,128)S(1)} %get-tuple-element.399), channel_id=1, source_target_pairs={{0,1},{1,2},{2,3},{3,4},{4,5},{5,6},{6,7},{8,9},{9,10},{10,11},{11... | collective-permute-start | bytes 46088 | tf_op jit(solution)/shard_map/ppermute | solution.py:21
  63.5 8.4 %collective-permute-start.7 = (f32[6,80,8]{2,1,0:T(8,128)S(1)}, f32[6,80,8]{2,1,0:T(8,128)S(1)}, u32[]{:S(2)}, u32[]{:S(2)}) collective-permute-start(f32[6,80,8]{2,1,0:T(8,128)S(1)} %get-tuple-element.400), channel_id=1, source_target_pairs={{1,0},{2,1},{3,2},{4,3},{5,4},{6,5},{7,6},{9,8},{10,9},{11,10},{12... | collective-permute-start | bytes 46088 | tf_op jit(solution)/shard_map/ppermute | solution.py:24
  65.0 7.7 %collective-permute-start.2 = (f32[7,80,8]{2,1,0:T(8,128)S(1)}, f32[7,80,8]{2,1,0:T(8,128)S(1)}, u32[]{:S(2)}, u32[]{:S(2)}) collective-permute-start(f32[7,80,8]{2,1,0:T(8,128)S(1)} %get-tuple-element.391), channel_id=1, source_target_pairs={{0,1},{1,2},{2,3},{3,4},{4,5},{5,6},{6,7},{8,9},{9,10},{10,11},{11... | collective-permute-start | bytes 53768 | tf_op jit(solution)/shard_map/ppermute | solution.py:21
  70.5 4.7 %collective-permute-start.3 = (f32[7,80,8]{2,1,0:T(8,128)S(1)}, f32[7,80,8]{2,1,0:T(8,128)S(1)}, u32[]{:S(2)}, u32[]{:S(2)}) collective-permute-start(f32[7,80,8]{2,1,0:T(8,128)S(1)} %get-tuple-element.392), channel_id=1, source_target_pairs={{1,0},{2,1},{3,2},{4,3},{5,4},{6,5},{7,6},{9,8},{10,9},{11,10},{12... | collective-permute-start | bytes 53768 | tf_op jit(solution)/shard_map/ppermute | solution.py:24
  93.3 5.1 %collective-permute-start.8 = (f32[6,8,256]{2,1,0:T(8,128)S(1)}, f32[6,8,256]{2,1,0:T(8,128)S(1)}, u32[]{:S(2)}, u32[]{:S(2)}) collective-permute-start(f32[6,8,256]{2,1,0:T(8,128)S(1)} %get-tuple-element.403), channel_id=1, source_target_pairs={{0,8},{8,16},{16,24},{1,9},{9,17},{17,25},{2,10},{10,18},{18,26},{... | collective-permute-start | bytes 147464 | tf_op jit(solution)/shard_map/ppermute | solution.py:21
  96.7 6.0 %collective-permute-start.9 = (f32[6,8,256]{2,1,0:T(8,128)S(1)}, f32[6,8,256]{2,1,0:T(8,128)S(1)}, u32[]{:S(2)}, u32[]{:S(2)}) collective-permute-start(f32[6,8,256]{2,1,0:T(8,128)S(1)} %get-tuple-element.404), channel_id=1, source_target_pairs={{8,0},{16,8},{24,16},{9,1},{17,9},{25,17},{10,2},{18,10},{26,18},{... | collective-permute-start | bytes 147464 | tf_op jit(solution)/shard_map/ppermute | solution.py:24
  102.8 8.2 %collective-permute-start.10 = (f32[6,80,8]{2,1,0:T(8,128)S(1)}, f32[6,80,8]{2,1,0:T(8,128)S(1)}, u32[]{:S(2)}, u32[]{:S(2)}) collective-permute-start(f32[6,80,8]{2,1,0:T(8,128)S(1)} %get-tuple-element.397), channel_id=1, source_target_pairs={{0,1},{1,2},{2,3},{3,4},{4,5},{5,6},{6,7},{8,9},{9,10},{10,11},{11... | collective-permute-start | bytes 46088 | tf_op jit(solution)/shard_map/ppermute | solution.py:21
  109.7 4.2 %collective-permute-start.11 = (f32[6,80,8]{2,1,0:T(8,128)S(1)}, f32[6,80,8]{2,1,0:T(8,128)S(1)}, u32[]{:S(2)}, u32[]{:S(2)}) collective-permute-start(f32[6,80,8]{2,1,0:T(8,128)S(1)} %get-tuple-element.398), channel_id=1, source_target_pairs={{1,0},{2,1},{3,2},{4,3},{5,4},{6,5},{7,6},{9,8},{10,9},{11,10},{12... | collective-permute-start | bytes 46088 | tf_op jit(solution)/shard_map/ppermute | solution.py:24
  122.3 47.4 %copy-start.13 = (f32[80,272]{1,0:T(8,128)S(1)}, f32[80,272]{1,0:T(8,128)}, u32[]{:S(2)}) copy-start(f32[80,272]{1,0:T(8,128)} %get-tuple-element.76) | copy-start | bytes 261124
  188.2 1.2 copy-start.33
  188.2 1.2 copy-start.34
  188.2 1.2 copy-start.35
  188.2 1.3 copy-start.36
  188.2 1.3 copy-start.37
  188.2 2.3 %copy-start.24 = (f32[80,272]{1,0:T(8,128)S(1)}, f32[80,272]{1,0:T(8,128)}, u32[]{:S(2)}) copy-start(f32[80,272]{1,0:T(8,128)} %get-tuple-element.185) | copy-start | bytes 261124
  188.3 2.3 %copy-start.25 = (f32[80,272]{1,0:T(8,128)S(1)}, f32[80,272]{1,0:T(8,128)}, u32[]{:S(2)}) copy-start(f32[80,272]{1,0:T(8,128)} %get-tuple-element.186) | copy-start | bytes 261124
  188.3 2.2 %copy-start.26 = (f32[80,272]{1,0:T(8,128)S(1)}, f32[80,272]{1,0:T(8,128)}, u32[]{:S(2)}) copy-start(f32[80,272]{1,0:T(8,128)} %get-tuple-element.141) | copy-start | bytes 261124
  (33 other events, 32.3 us)
where the time goes:
time: 194 us; the launch traced here: 193 us
  blocking collectives  88.2 us (45%)
  other arithmetic  43.6 us (22%)
  starting transfers between devices  33.4 us (17%)
  local copies, waits for them, and re-layouts  10.8 us (6%)
  waiting for transfers between devices  10.1 us (5%)
  between operations  6.78 us (3%)
    psum x2, blocking collectives, on_device(): lax.psum((local_misfit, local_scale), ('gy', 'gx'))  88.2 us
    ppermute x6, starting transfers between devices, padded_2(): lax.ppermute(lax.slice_in_dim(block, block.shape[dim] - width, None, axis...  25.7 us
    ppermute x6, waiting for transfers between devices, padded_2(): lax.ppermute(lax.slice_in_dim(block, 0, width, axis=dim), axis, backward)  9.64 us
    add_any x6, other arithmetic, sweep_core(): thick_mid + shifted(thick_pad, row_offset, col_offset)  8.05 us
    ppermute x6, starting transfers between devices, padded_2(): lax.ppermute(lax.slice_in_dim(block, 0, width, axis=dim), axis, backward)  7.74 us
    unnamed x90, local copies, waits for them, and re-layouts  7.3 us
    reduce_sum x5, other arithmetic, sweep_core(): residual = forcing - friction * center + flux_sum  4.75 us
  transfers between devices with their start and end apart: 12, of which 4 were waited for; matrix products, arithmetic and copies ran while one was open for 1% of the time, Pallas kernels for 0%

commit v1 on v0

v1 whole, which is shorter than its diff:
```python
import jax
import jax.numpy as jnp
from jax import lax
from jax.experimental import pallas as pl
from jax.experimental.pallas import tpu as pltpu
from jax.sharding import PartitionSpec as P

RELAXATION = 0.8
TIME_STEP = 0.1
EPSILON = 1e-06
MESH = pl.DeviceIdType.MESH

RIM = 2
COLS = 16

MASK, BETA, SLU, SLV, H1, U1, V1 = range(7)
DEEP = 7
FLAGS, H0, U0, V0, OU0, OV0, OU1, OV1, ADJ = range(7, 16)
FIELDS = 16

STATIC = ("cov", "gr", "fri", "cce", "ccs", "de", "ds")
STEP = ("ce", "cs", "u1", "v1", "u2", "v2", "u3", "v3")
SWEEP = ("pe", "ps", "deu", "dev", "dsu", "dsv", "yu", "yv", "inv")
BACK = ("qu", "qv", "e", "bu", "bv")
REST = ("hce", "hcs", "hacc", "facc", "g1", "f1", "g0", "f0")


def scratch_names():
    names = list(STATIC)
    for n in range(2):
        names += [f"{n}{name}" for name in STEP]
        for j in range(3):
            names += [f"{n}{j}{name}" for name in SWEEP]
    for b in range(2):
        names += [f"b{b}{name}" for name in BACK]
    return names + list(REST)


NAMES = scratch_names()


def make_kernel(ny, nx, rows, cols, cell_count):
    strips = rows // 8
    total = strips + 2 * RIM
    first, last = RIM - 1, RIM + strips + 1
    width = cols + 128

    def kernel(
        thick_hbm, vel_hbm, slope_hbm, beta_hbm, mask_hbm, flags_hbm, obs_hbm, adj_hbm,
        beta_out, thick_out, misfit_out,
        fld, col_send, col_recv, sum_x, sum_y, send_sem, recv_sem,
        sx_send, sx_recv, sy_send, sy_recv, in_sem,
        thick_in, vel_in, slope_in, beta_in, mask_in, flags_in, obs_in, adj_in, *refs,
    ):
        pairs = (
            (mask_hbm, mask_in), (beta_hbm, beta_in), (slope_hbm, slope_in), (thick_hbm, thick_in),
            (vel_hbm, vel_in), (flags_hbm, flags_in), (obs_hbm, obs_in), (adj_hbm, adj_in),
        )
        loads = [
            pltpu.make_async_copy(src, dst, in_sem.at[i]) for i, (src, dst) in enumerate(pairs)
        ]
        for load in loads:
            load.start()
        s = dict(zip(NAMES, refs))
        gy, gx = lax.axis_index("gy"), lax.axis_index("gx")
        centre = slice(RIM, RIM + strips)

        def exists(dy, dx):
            ok = None
            for move, at, count in ((dy, gy, ny), (dx, gx, nx)):
                if move:
                    here = at > 0 if move < 0 else at < count - 1
                    ok = here if ok is None else jnp.logical_and(ok, here)
            return ok

        diagonals = ((-1, -1), (-1, 1), (1, -1), (1, 1))
        sides = ((-1, 0), (1, 0), (0, -1), (0, 1))

        zero_rows = jnp.zeros((FIELDS, 2, 8, cols), jnp.float32)
        fld[:, 0:RIM, :, 0:cols] = zero_rows
        fld[:, RIM + strips : total, :, 0:cols] = zero_rows
        col_recv[...] = jnp.zeros_like(col_recv)

        barrier = pltpu.get_barrier_semaphore()
        for off in range(1, nx):
            pl.semaphore_signal(
                barrier, inc=1, device_id=(gy, lax.rem(gx + off, nx)), device_id_type=MESH
            )
        for off in range(1, ny):
            pl.semaphore_signal(
                barrier, inc=1, device_id=(lax.rem(gy + off, ny), gx), device_id_type=MESH
            )
        for dy, dx in diagonals:

            @pl.when(exists(dy, dx))
            def _():
                pl.semaphore_signal(
                    barrier, inc=1, device_id=(gy + dy, gx + dx), device_id_type=MESH
                )

        def place(field, value):
            fld[field, centre, :, 0:cols] = value.astype(jnp.float32).reshape(strips, 8, cols)

        for load in loads:
            load.wait()
        place(MASK, mask_in[...])
        place(BETA, beta_in[...])
        place(SLU, slope_in[0])
        place(SLV, slope_in[1])
        place(H1, thick_in[1])
        place(U1, vel_in[1, 0])
        place(V1, vel_in[1, 1])
        place(FLAGS, flags_in[...])
        place(H0, thick_in[0])
        place(U0, vel_in[0, 0])
        place(V0, vel_in[0, 1])
        place(OU0, obs_in[0, 0])
        place(OV0, obs_in[0, 1])
        place(OU1, obs_in[1, 0])
        place(OV1, obs_in[1, 1])
        place(ADJ, adj_in[...])

        lane = lax.broadcasted_iota(jnp.int32, (8, 128), 1)
        sub = lax.broadcasted_iota(jnp.int32, (8, width), 0)

        for n, (ou, ov) in enumerate(((OU0, OV0), (OU1, OV1))):
            def scale_body(k, acc, ou=ou, ov=ov):
                a, b = fld[ou, k, :, 0:cols], fld[ov, k, :, 0:cols]
                t = jnp.where(fld[MASK, k, :, 0:cols] == 2.0, a * a + b * b, 0.0)
                for c in range(0, cols, 128):
                    acc = acc + t[:, c : c + 128]
                return acc

            sum_x[0, 0, n] = lax.fori_loop(
                RIM, RIM + strips, scale_body, jnp.zeros((8, 128), jnp.float32)
            )

        def pack_body(k, _):
            for side, at in ((0, 0), (1, cols - 128)):
                for tile in range(FIELDS * COLS // 128):
                    packed = jnp.zeros((8, 128), jnp.float32)
                    for i in range(128 // COLS):
                        x = fld[tile * (128 // COLS) + i, k + RIM, :, at : at + 128]
                        move = (i * COLS - (0 if side == 0 else 128 - COLS)) % 128
                        if move:
                            x = pltpu.roll(x, move, 1)
                        inside = jnp.logical_and(lane >= i * COLS, lane < (i + 1) * COLS)
                        packed = jnp.where(inside, x, packed)
                    col_send[side, k, :, tile * 128 : (tile + 1) * 128] = packed
            return 0

        lax.fori_loop(0, strips, pack_body, 0)

        beside = [
            jnp.where(at > 0, 1, 0) + jnp.where(at < count - 1, 1, 0)
            for at, count in ((gy, ny), (gx, nx))
        ]
        pl.semaphore_wait(barrier, (nx - 1) + (ny - 1) + beside[0] * beside[1])

        hi = RIM + strips
        plan = []
        for i, (dy, dx) in enumerate(sides):
            if dy:
                src = slice(RIM, RIM + 2) if dy < 0 else slice(hi - 2, hi)
                dst = slice(hi, hi + 2) if dy < 0 else slice(0, 2)
                plan.append(
                    (dy, dx, fld.at[0:DEEP, src, :, 0:cols], fld.at[0:DEEP, dst, :, 0:cols])
                )
                src = slice(RIM, RIM + 1) if dy < 0 else slice(hi - 1, hi)
                dst = slice(hi, hi + 1) if dy < 0 else slice(1, 2)
                plan.append(
                    (dy, dx, fld.at[DEEP:FIELDS, src, :, 0:cols], fld.at[DEEP:FIELDS, dst, :, 0:cols])
                )
            else:
                side = 0 if dx < 0 else 1
                plan.append((dy, dx, col_send.at[side], col_recv.at[side, centre]))
        for dy, dx in diagonals:
            side = 0 if dx < 0 else 1
            src = slice(0, 2) if dy < 0 else slice(strips - 2, strips)
            dst = slice(hi, hi + 2) if dy < 0 else slice(0, 2)
            plan.append((dy, dx, col_send.at[side, src], col_recv.at[side, dst]))
        copies = []
        for i, (dy, dx, src, dst) in enumerate(plan):
            copy = pltpu.make_async_remote_copy(
                src_ref=src, dst_ref=dst, send_sem=send_sem.at[i], recv_sem=recv_sem.at[i],
                device_id=(gy + dy, gx + dx), device_id_type=MESH,
            )
            copies.append((dy, dx, copy))

            @pl.when(exists(dy, dx))
            def _():
                copy.start()

        def spread(which, axis):
            buf, ssem, rsem, count = (
                (sum_x, sx_send, sx_recv, nx) if axis == "gx" else (sum_y, sy_send, sy_recv, ny)
            )
            made = []
            for off in range(1, count):
                peer = (
                    (gy, lax.rem(gx + off, nx)) if axis == "gx" else (lax.rem(gy + off, ny), gx)
                )
                made.append(
                    pltpu.make_async_remote_copy(
                        src_ref=buf.at[which, 0], dst_ref=buf.at[which, off],
                        send_sem=ssem.at[which, off], recv_sem=rsem.at[which, off],
                        device_id=peer, device_id_type=MESH,
                    )
                )
            return made

        def added(which, axis, n):
            buf, me, count = (sum_x, gx, nx) if axis == "gx" else (sum_y, gy, ny)
            acc = jnp.zeros((8, 128), jnp.float32)
            for src in range(count):
                acc = acc + buf[which, lax.rem(me - src + count, count), n]
            return acc

        def whole(tile):
            return jnp.sum(jnp.sum(tile, axis=1, keepdims=True), axis=0, keepdims=True)

        scale_x = spread(0, "gx")
        for copy in scale_x:
            copy.start()

        for copy in scale_x:
            copy.wait()
        for n in range(2):
            sum_y[0, 0, n] = added(0, "gx", n)
        scale_y = spread(0, "gy")
        for copy in scale_y:
            copy.start()

        for dy, dx, copy in copies:

            @pl.when(exists(-dy, -dx))
            def _():
                copy.wait_recv()

        def unpack_body(k, _):
            for tile in range(FIELDS * COLS // 128):
                nxt = col_recv[0, k, :, tile * 128 : (tile + 1) * 128]
                prv = col_recv[1, k, :, tile * 128 : (tile + 1) * 128]
                for i in range(128 // COLS):
                    a = pltpu.roll(nxt, (-i * COLS) % 128, 1) if i else nxt
                    move = (128 - COLS - i * COLS) % 128
                    b = pltpu.roll(prv, move, 1) if move else prv
                    both = jnp.where(lane < COLS, a, jnp.where(lane >= 128 - COLS, b, 0.0))
                    fld[tile * (128 // COLS) + i, k, :, cols:width] = both
            return 0

        lax.fori_loop(0, total, unpack_body, 0)

        def east(x):
            return pltpu.roll(x, width - 1, 1)

        def west(x):
            return pltpu.roll(x, 1, 1)

        def south(cur, nxt):
            return pltpu.roll(jnp.where(sub == 0, nxt, cur), 7, 0)

        def north(prev, cur):
            return pltpu.roll(jnp.where(sub == 7, prev, cur), 1, 0)

        zero = jnp.zeros((8, width), jnp.float32)

        def after(k):
            return jnp.minimum(k + 1, total - 1)

        def static_body(k, _):
            mask = fld[MASK, k]
            cov = jnp.where(mask > 0.0, 1.0, 0.0)
            cov_n = jnp.where(fld[MASK, after(k)] > 0.0, 1.0, 0.0)
            gr = jnp.where(mask == 2.0, 1.0, 0.0)
            cce = 0.5 * cov * east(cov)
            ccs = 0.5 * cov * south(cov, cov_n)
            flags = fld[FLAGS, k]
            ds = jnp.where(flags >= 2.0, 1.0, 0.0)
            s["cov"][k] = cov
            s["gr"][k] = gr
            s["fri"][k] = fld[BETA, k] * gr
            s["cce"][k] = cce
            s["ccs"][k] = ccs
            s["ds"][k] = ds
            s["de"][k] = flags - 2.0 * ds
            for n, h in ((0, H0), (1, H1)):
                hh = fld[h, k]
                s[f"{n}ce"][k] = cce * (hh + east(hh))
                s[f"{n}cs"][k] = ccs * (hh + south(hh, fld[h, after(k)]))
            return 0

        lax.fori_loop(0, total, static_body, 0)

        H = (H0, H1)
        W = ((U0, V0), (U1, V1))

        def velocity(n, j):
            if j == 0:
                return fld.at[W[n][0]], fld.at[W[n][1]]
            return s[f"{n}u{j}"], s[f"{n}v{j}"]

        def edge_zero(names):
            for name in names:
                for k in (first - 1, last):
                    s[name][k] = zero

        edge_zero([f"{n}{c}{j}" for n in range(2) for j in (1, 2, 3) for c in "uv"])
        edge_zero([f"b{b}{c}" for b in range(2) for c in ("qu", "qv", "e")] + ["g1"])

        def forward(n, j, lo, end):
            u_ref, v_ref = velocity(n, j)
            u_to, v_to = velocity(n, j + 1)
            t = {name: s[f"{n}{j}{name}"] for name in SWEEP}

            def body(k, carry):
                pfu, pfv, pc = carry
                kn = after(k)
                u, v = u_ref[k], v_ref[k]
                deu, dev = east(u) - u, east(v) - v
                dsu, dsv = south(u, u_ref[kn]) - u, south(v, v_ref[kn]) - v
                pe = jnp.exp(jnp.log(1.0 + (deu * deu + dev * dev)) * (-1.0 / 3.0))
                ps = jnp.exp(jnp.log(1.0 + (dsu * dsu + dsv * dsv)) * (-1.0 / 3.0))
                ce, cs = s[f"{n}ce"][k] * pe, s[f"{n}cs"][k] * ps
                feu, fev, fsu, fsv = ce * deu, ce * dev, cs * dsu, cs * dsv
                fri, h = s["fri"][k], fld[H[n], k]
                inv = 1.0 / (1.0 + fri + ((ce + west(ce)) + (cs + north(pc, cs))))
                ru = h * fld[SLU, k] - fri * u + ((feu - west(feu)) + (fsu - north(pfu, fsu)))
                rv = h * fld[SLV, k] - fri * v + ((fev - west(fev)) + (fsv - north(pfv, fsv)))
                yu, yv = ru * inv, rv * inv
                cov = s["cov"][k]
                u_to[k] = cov * (u + RELAXATION * yu)
                v_to[k] = cov * (v + RELAXATION * yv)
                for name, value in zip(SWEEP, (pe, ps, deu, dev, dsu, dsv, yu, yv, inv)):
                    t[name][k] = value
                return fsu, fsv, cs

            lax.fori_loop(lo, end, body, (zero, zero, zero))

        forward(1, 0, 0, total)
        forward(1, 1, first, last)
        forward(1, 2, first, last)
        forward(0, 0, first, last)
        forward(0, 1, first, last)
        forward(0, 2, first, last)

        O = ((OU0, OV0), (OU1, OV1))
        for n in range(2):
            def misfit_body(k, acc, n=n):
                a = s[f"{n}u3"][k, :, 0:cols] - fld[O[n][0], k, :, 0:cols]
                b = s[f"{n}v3"][k, :, 0:cols] - fld[O[n][1], k, :, 0:cols]
                t = s["gr"][k, :, 0:cols] * (a * a + b * b)
                for c in range(0, cols, 128):
                    acc = acc + t[:, c : c + 128]
                return acc

            sum_x[1, 0, n] = 0.5 * lax.fori_loop(
                RIM, RIM + strips, misfit_body, jnp.zeros((8, 128), jnp.float32)
            )
        misfit_x = spread(1, "gx")
        for copy in misfit_x:
            copy.start()

        for copy in scale_y:
            copy.wait()
        scales = [whole(added(0, "gy", n)) * (1.0 / cell_count) + EPSILON for n in range(2)]

        def emit(n, j, b, k, lu, lv):
            cov, fri = s["cov"][k], s["fri"][k]
            au, av = cov * lu, cov * lv
            inv = RELAXATION * s[f"{n}{j}inv"][k]
            qu, qv = au * inv, av * inv
            s[f"b{b}qu"][k] = qu
            s[f"b{b}qv"][k] = qv
            s[f"b{b}e"][k] = -(qu * s[f"{n}{j}yu"][k] + qv * s[f"{n}{j}yv"][k])
            s[f"b{b}bu"][k] = au - fri * qu
            s[f"b{b}bv"][k] = av - fri * qv

        def transport(n, g_ref):
            per_scale = jnp.broadcast_to(1.0 / scales[n], (8, width))

            def body(k, carry):
                pvs, phs = carry
                kn = k + 1
                g, gn = s["cov"][k] * g_ref[k], s["cov"][kn] * g_ref[kn]
                h, hn = fld[H[n], k], fld[H[n], kn]
                u, v = s[f"{n}u3"][k], s[f"{n}v3"][k]
                de, ds = s["de"][k], s["ds"][k]
                pse = (TIME_STEP * s["cce"][k]) * (east(g) - g)
                pss = (TIME_STEP * s["ccs"][k]) * (south(g, gn) - g)
                ue = pse * (de * h + (1.0 - de) * east(h))
                vs = pss * (ds * h + (1.0 - ds) * south(h, hn))
                he = pse * (u + east(u))
                hs = pss * (v + south(v, s[f"{n}v3"][kn]))
                he_here, hs_here = de * he, ds * hs
                he_there, hs_there = he - he_here, hs - hs_here
                seed = s["gr"][k] * per_scale
                lu = seed * (u - fld[O[n][0], k]) + (ue + west(ue))
                lv = seed * (v - fld[O[n][1], k]) + (vs + north(pvs, vs))
                s["hacc"][k] = g + (he_here + west(he_there)) + (hs_here + north(phs, hs_there))
                emit(n, 2, 0, k, lu, lv)
                return vs, hs_there

            lax.fori_loop(first, last, body, (zero, zero))

        def backward(n, j, b, end, g_to=None, f_to=None):
            u_ref, v_ref = velocity(n, j)
            t = {name: s[f"{n}{j}{name}"] for name in SWEEP}
            q = {name: s[f"b{b}{name}"] for name in BACK}
            start, finish = j == 2, j == 0

            def body(k, carry):
                kn = k + 1
                qu, qv, e = q["qu"][k], q["qv"][k], q["e"][k]
                feu, fev = qu - east(qu), qv - east(qv)
                fsu, fsv = qu - south(qu, q["qu"][kn]), qv - south(qv, q["qv"][kn])
                pe, ps = t["pe"][k], t["ps"][k]
                deu, dev, dsu, dsv = t["deu"][k], t["dev"][k], t["dsu"][k], t["dsv"][k]
                ke = (feu * deu + fev * dev) + (e + east(e))
                ks = (fsu * dsu + fsv * dsv) + (e + south(e, q["e"][kn]))
                kpe, kps = ke * pe, ks * ps
                f = e - (qu * u_ref[k] + qv * v_ref[k])
                h = qu * fld[SLU, k] + qv * fld[SLV, k] + s["hacc"][k]
                if not start:
                    kpe_sum, kps_sum = s["hce"][k] + kpe, s["hcs"][k] + kps
                    f = f + s["facc"][k]
                else:
                    kpe_sum, kps_sum = kpe, kps
                if finish:
                    ge, gs = s["cce"][k] * kpe_sum, s["ccs"][k] * kps_sum
                    g_to[k] = h + ((ge + west(ge)) + (gs + north(carry[0], gs)))
                    f_to[k] = f
                    return (gs,)
                s["hce"][k] = kpe_sum
                s["hcs"][k] = kps_sum
                s["facc"][k] = f
                s["hacc"][k] = h
                ce, cs = s[f"{n}ce"][k] * pe, s[f"{n}cs"][k] * ps
                te = (2.0 / 3.0) * ce * (pe * pe) * kpe
                ts = (2.0 / 3.0) * cs * (ps * ps) * kps
                xeu, xev = ce * feu - te * deu, ce * fev - te * dev
                xsu, xsv = cs * fsu - ts * dsu, cs * fsv - ts * dsv
                lu = q["bu"][k] + ((west(xeu) - xeu) + (north(carry[0], xsu) - xsu))
                lv = q["bv"][k] + ((west(xev) - xev) + (north(carry[1], xsv) - xsv))
                emit(n, j - 1, 1 - b, k, lu, lv)
                return xsu, xsv

            lax.fori_loop(first, end, body, (zero,) if finish else (zero, zero))

        transport(1, fld.at[ADJ])
        backward(1, 2, 0, last)
        backward(1, 1, 1, last)
        backward(1, 0, 0, last, s["g1"], s["f1"])

        for copy in misfit_x:
            copy.wait()
        for n in range(2):
            sum_y[1, 0, n] = added(1, "gx", n)
        misfit_y = spread(1, "gy")
        for copy in misfit_y:
            copy.start()

        transport(0, s["g1"])
        backward(0, 2, 0, last)
        backward(0, 1, 1, last)
        backward(0, 0, 0, last - 1, s["g0"], s["f0"])

        f_sum = s["f1"][centre, :, 0:cols] + s["f0"][centre, :, 0:cols]
        beta_out[...] = s["gr"][centre, :, 0:cols] * f_sum
        thick_out[...] = s["g0"][centre, :, 0:cols]

        for copy in misfit_y:
            copy.wait()
        parts = [whole(added(1, "gy", n)) * (1.0 / cell_count) / scales[n] for n in range(2)]
        misfit_out[...] = parts[1] + parts[0]
        for dy, dx, copy in copies:

            @pl.when(exists(dy, dx))
            def _():
                copy.wait_send()

    return kernel


def on_device(*args):
    ny, nx = lax.axis_size("gy"), lax.axis_size("gx")
    rows, cols = args[3].shape
    strips = rows // 8
    total = strips + 2 * RIM
    width = cols + 128
    vmem = pl.BlockSpec(memory_space=pltpu.VMEM)
    dma = pltpu.SemaphoreType.DMA
    beta, thick, misfit = pl.pallas_call(
        make_kernel(ny, nx, rows, cols, rows * cols * ny * nx),
        out_shape=(
            jax.ShapeDtypeStruct((strips, 8, cols), jnp.float32),
            jax.ShapeDtypeStruct((strips, 8, cols), jnp.float32),
            jax.ShapeDtypeStruct((1, 1), jnp.float32),
        ),
        in_specs=[pl.BlockSpec(memory_space=pltpu.HBM)] * len(args),
        out_specs=(vmem, vmem, vmem),
        scratch_shapes=[
            pltpu.VMEM((FIELDS, total, 8, width), jnp.float32),
            pltpu.VMEM((2, strips, 8, FIELDS * COLS), jnp.float32),
            pltpu.VMEM((2, total, 8, FIELDS * COLS), jnp.float32),
            pltpu.VMEM((2, nx, 2, 8, 128), jnp.float32),
            pltpu.VMEM((2, ny, 2, 8, 128), jnp.float32),
            dma((10,)), dma((10,)),
            dma((2, nx)), dma((2, nx)), dma((2, ny)), dma((2, ny)), dma((len(args),)),
        ]
        + [pltpu.VMEM(arg.shape, arg.dtype) for arg in args]
        + [pltpu.VMEM((total, 8, width), jnp.float32)] * len(NAMES),
        compiler_params=pltpu.CompilerParams(
            collective_id=0, has_side_effects=True, vmem_limit_bytes=62 * 1024 * 1024
        ),
    )(*args)
    return beta.reshape(rows, cols), thick.reshape(rows, cols), misfit.reshape(())


def solution(mesh):
    in_specs = (
        P(None, "gy", "gx"),
        P(None, None, "gy", "gx"),
        P(None, "gy", "gx"),
        P("gy", "gx"),
        P("gy", "gx"),
        P("gy", "gx"),
        P(None, None, "gy", "gx"),
        P("gy", "gx"),
    )
    out_specs = (P("gy", "gx"), P("gy", "gx"), P())
    return jax.shard_map(
        on_device, mesh=mesh, in_specs=in_specs, out_specs=out_specs, check_vma=False
    )
```

time: 194 us -> 43.8 us (0.23)
  blocking collectives: 88.2 us -> 0 us
  other arithmetic: 43.6 us -> 0 us
  Pallas kernels: 0 us -> 38.6 us
  starting transfers between devices: 33.4 us -> 0 us
  waiting for transfers between devices: 10.1 us -> 0 us
  local copies, waits for them, and re-layouts: 10.8 us -> 2.14 us
  between operations: 6.78 us -> 2.41 us
    psum x2 -> x0, blocking collectives: 88.2 us -> none  [on_device(): lax.psum((local_misfit, local_scale), ('gy', 'gx'))]
    pallas_call x0 -> x1, Pallas kernels: none -> 38.6 us  [on_device(): pl.pallas_call(make_kernel(ny, nx, rows, cols, rows * cols * ny * nx), ou...]
    ppermute x12 -> x0, starting transfers between devices: 33.4 us -> none  [the longest x6 25.7 us: padded_2(): lax.ppermute(lax.slice_in_dim(block, block.shape[dim] - width, None, axis...]
    add_any x20 -> x0, other arithmetic: 12.5 us -> none  [the longest x6 8.05 us: sweep_core(): thick_mid + shifted(thick_pad, row_offset, col_offset)]
    reduce_sum x24 -> x0, other arithmetic: 11.7 us -> none  [the longest x5 4.75 us: sweep_core(): residual = forcing - friction * center + flux_sum]
    ppermute x12 -> x0, waiting for transfers between devices: 10.1 us -> none  [the longest x6 9.64 us: padded_2(): lax.ppermute(lax.slice_in_dim(block, 0, width, axis=dim), axis, backward)]
    mul x26 -> x0, other arithmetic: 9.32 us -> none  [the longest x8 3.25 us: sweep_core(): flux_sum = flux_sum + coupling * difference]
    unnamed x90 -> x4, local copies, waits for them, and re-layouts: 7.3 us -> 2.14 us
  transfers between devices with their start and end apart: 12 -> 0, of which waited for: 4 -> 0; matrix products, arithmetic and copies ran while one was open for 1% -> 0% of each run, Pallas kernels for 0% -> 0%
where the time goes in v1:
time: 43.8 us; the launch traced here: 43.1 us
  Pallas kernels  38.6 us (88%)
  between operations  2.41 us (6%)
  local copies, waits for them, and re-layouts  2.14 us (5%)
    pallas_call x1, Pallas kernels, on_device(): pl.pallas_call(make_kernel(ny, nx, rows, cols, rows * cols * ny * nx), ou...  38.6 us
    unnamed x4, local copies, waits for them, and re-layouts  2.14 us

profile of v1, /device:TPU:0, one launch (start us, length us, event | category | flops | bytes accessed | tf_op | source)
XLA Modules:
  0.0 43.1 jit_solution(11547902257541596243)
XLA Ops:
  0.6 38.6 %shard_map.103 = (f32[8,8,256]{2,1,0:T(8,128)}, f32[8,8,256]{2,1,0:T(8,128)}, f32[1,1]{1,0:T(1,128)}) custom-call(bf16[2,64,256]{2,1,0:T(8,128)(2,1)} %thick_hbm.1, bf16[2,2,64,256]{3,2,1,0:T(8,128)(2,1)} %vel_hbm.1, bf16[2,64,256]{2,1,0:T(8,128)(2,1)} %slope_hbm.1, f32[64,256]{1,0:T(8,128)} %beta_hbm.1, s32[64,256]{1,0:T(8,128)} %mask_hbm.1, ...), custom_call_target="tpu_custom_call" | custom-call | tf_op jit(solution)/shard_map/pallas_call | solution.py:493
  39.2 0.0 copy-start
  39.2 1.5 %copy.14 = f32[64,256]{1,0:T(8,128)} copy(f32[64,256]{1,0:T(8,128)} %bitcast.4) | data formatting | bytes 131072
  40.7 0.0 copy-done
  40.7 0.6 %copy.15 = f32[64,256]{1,0:T(8,128)} copy(f32[64,256]{1,0:T(8,128)S(1)} %bitcast.3) | data formatting | bytes 131072
Async XLA Ops:
  39.2 1.5 %copy-start = (f32[8,8,256]{2,1,0:T(8,128)S(1)}, f32[8,8,256]{2,1,0:T(8,128)}, u32[]{:S(2)}) copy-start(f32[8,8,256]{2,1,0:T(8,128)} %get-tuple-element.7) | copy-start | bytes 196612

commit v2 on v1

--- a/solution.py
+++ b/solution.py
@@ -48,7 +48,7 @@
     def kernel(
         thick_hbm, vel_hbm, slope_hbm, beta_hbm, mask_hbm, flags_hbm, obs_hbm, adj_hbm,
         beta_out, thick_out, misfit_out,
-        fld, col_send, col_recv, sum_x, sum_y, send_sem, recv_sem,
+        fld, col_send, col_recv, row_send, row_recv, sum_x, sum_y, send_sem, recv_sem,
         sx_send, sx_recv, sy_send, sy_recv, in_sem,
         thick_in, vel_in, slope_in, beta_in, mask_in, flags_in, obs_in, adj_in, *refs,
     ):
@@ -80,6 +80,7 @@
         fld[:, 0:RIM, :, 0:cols] = zero_rows
         fld[:, RIM + strips : total, :, 0:cols] = zero_rows
         col_recv[...] = jnp.zeros_like(col_recv)
+        row_recv[...] = jnp.zeros_like(row_recv)
 
         barrier = pltpu.get_barrier_semaphore()
         for off in range(1, nx):
@@ -101,7 +102,12 @@
         def place(field, value):
             fld[field, centre, :, 0:cols] = value.astype(jnp.float32).reshape(strips, 8, cols)
 
-        for load in loads:
+        lane = lax.broadcasted_iota(jnp.int32, (8, 128), 1)
+        sub = lax.broadcasted_iota(jnp.int32, (8, width), 0)
+        sub_own = lax.broadcasted_iota(jnp.int32, (8, cols), 0)
+        hi = RIM + strips
+
+        for load in loads[:5]:
             load.wait()
         place(MASK, mask_in[...])
         place(BETA, beta_in[...])
@@ -110,7 +116,105 @@
         place(H1, thick_in[1])
         place(U1, vel_in[1, 0])
         place(V1, vel_in[1, 1])
+
+        for up in range(2):
+            at, row = (RIM + 1, 0) if up else (hi - 2, 6)
+            for strip in range(2):
+                packed = jnp.zeros((8, cols), jnp.float32)
+                for i in range(min(4, DEEP - 4 * strip)):
+                    x = fld[4 * strip + i, at, :, 0:cols]
+                    move = (2 * i - row) % 8
+                    if move:
+                        x = pltpu.roll(x, move, 0)
+                    inside = jnp.logical_and(sub_own >= 2 * i, sub_own < 2 * i + 2)
+                    packed = jnp.where(inside, x, packed)
+                row_send[up, strip] = packed
+
+        beside = [
+            jnp.where(at > 0, 1, 0) + jnp.where(at < count - 1, 1, 0)
+            for at, count in ((gy, ny), (gx, nx))
+        ]
+        pl.semaphore_wait(barrier, (nx - 1) + (ny - 1) + beside[0] * beside[1])
+
+        def begin(plan, base):
+            copies = []
+            for i, (dy, dx, src, dst) in enumerate(plan):
+                copy = pltpu.make_async_remote_copy(
+                    src_ref=src, dst_ref=dst,
+                    send_sem=send_sem.at[base + i], recv_sem=recv_sem.at[base + i],
+                    device_id=(gy + dy, gx + dx), device_id_type=MESH,
+                )
+                copies.append((dy, dx, copy))
+
+                @pl.when(exists(dy, dx))
+                def _():
+                    copy.start()
+
+            return copies
+
+        def arrived(copies):
+            for dy, dx, copy in copies:
+
+                @pl.when(exists(-dy, -dx))
+                def _():
+                    copy.wait_recv()
+
+        def row_plan(fields):
+            return [
+                (-1, 0, fld.at[fields, RIM, :, 0:cols], fld.at[fields, hi, :, 0:cols]),
+                (1, 0, fld.at[fields, hi - 1, :, 0:cols], fld.at[fields, RIM - 1, :, 0:cols]),
+            ]
+
+        def col_plan(tile):
+            send, recv = col_send.at[tile], col_recv.at[tile]
+            plan = []
+            for side, dx in ((0, -1), (1, 1)):
+                plan.append((0, dx, send.at[side], recv.at[side, centre]))
+                plan.append((-1, dx, send.at[side, 0:2], recv.at[side, hi : hi + 2]))
+                plan.append((1, dx, send.at[side, strips - 2 : strips], recv.at[side, 0:2]))
+            return plan
+
+        per_tile = 128 // COLS
+
+        def pack(tile):
+            def pack_body(k, _):
+                for side, at in ((0, 0), (1, cols - 128)):
+                    packed = jnp.zeros((8, 128), jnp.float32)
+                    for i in range(per_tile):
+                        x = fld[tile * per_tile + i, k + RIM, :, at : at + 128]
+                        move = (i * COLS - (0 if side == 0 else 128 - COLS)) % 128
+                        if move:
+                            x = pltpu.roll(x, move, 1)
+                        inside = jnp.logical_and(lane >= i * COLS, lane < (i + 1) * COLS)
+                        packed = jnp.where(inside, x, packed)
+                    col_send[tile, side, k] = packed
+                return 0
+
+            lax.fori_loop(0, strips, pack_body, 0, unroll=2)
+
+        def unpack(tile):
+            def unpack_body(k, _):
+                nxt, prv = col_recv[tile, 0, k], col_recv[tile, 1, k]
+                for i in range(per_tile):
+                    a = pltpu.roll(nxt, (-i * COLS) % 128, 1) if i else nxt
+                    move = (128 - COLS - i * COLS) % 128
+                    b = pltpu.roll(prv, move, 1) if move else prv
+                    both = jnp.where(lane < COLS, a, jnp.where(lane >= 128 - COLS, b, 0.0))
+                    fld[tile * per_tile + i, k, :, cols:width] = both
+                return 0
+
+            lax.fori_loop(0, total, unpack_body, 0, unroll=2)
+
+        near = begin(
+            row_plan(slice(0, DEEP))
+            + [(-1, 0, row_send.at[1], row_recv.at[1]), (1, 0, row_send.at[0], row_recv.at[0])],
+            0,
+        )
+        for load in loads[5:]:
+            load.wait()
         place(FLAGS, flags_in[...])
+        pack(0)
+        near += begin(col_plan(0), 4)
         place(H0, thick_in[0])
         place(U0, vel_in[0, 0])
         place(V0, vel_in[0, 1])
@@ -119,9 +223,9 @@
         place(OU1, obs_in[1, 0])
         place(OV1, obs_in[1, 1])
         place(ADJ, adj_in[...])
-
-        lane = lax.broadcasted_iota(jnp.int32, (8, 128), 1)
-        sub = lax.broadcasted_iota(jnp.int32, (8, width), 0)
+        far = begin(row_plan(slice(DEEP, FIELDS)), 10)
+        pack(1)
+        far += begin(col_plan(1), 12)
 
         for n, (ou, ov) in enumerate(((OU0, OV0), (OU1, OV1))):
             def scale_body(k, acc, ou=ou, ov=ov):
@@ -132,64 +236,8 @@
                 return acc
 
             sum_x[0, 0, n] = lax.fori_loop(
-                RIM, RIM + strips, scale_body, jnp.zeros((8, 128), jnp.float32)
+                RIM, RIM + strips, scale_body, jnp.zeros((8, 128), jnp.float32), unroll=2
             )
-
-        def pack_body(k, _):
-            for side, at in ((0, 0), (1, cols - 128)):
-                for tile in range(FIELDS * COLS // 128):
-                    packed = jnp.zeros((8, 128), jnp.float32)
-                    for i in range(128 // COLS):
-                        x = fld[tile * (128 // COLS) + i, k + RIM, :, at : at + 128]
-                        move = (i * COLS - (0 if side == 0 else 128 - COLS)) % 128
-                        if move:
-                            x = pltpu.roll(x, move, 1)
-                        inside = jnp.logical_and(lane >= i * COLS, lane < (i + 1) * COLS)
-                        packed = jnp.where(inside, x, packed)
-                    col_send[side, k, :, tile * 128 : (tile + 1) * 128] = packed
-            return 0
-
-        lax.fori_loop(0, strips, pack_body, 0)
-
-        beside = [
-            jnp.where(at > 0, 1, 0) + jnp.where(at < count - 1, 1, 0)
-            for at, count in ((gy, ny), (gx, nx))
-        ]
-        pl.semaphore_wait(barrier, (nx - 1) + (ny - 1) + beside[0] * beside[1])
-
-        hi = RIM + strips
-        plan = []
-        for i, (dy, dx) in enumerate(sides):
-            if dy:
-                src = slice(RIM, RIM + 2) if dy < 0 else slice(hi - 2, hi)
-                dst = slice(hi, hi + 2) if dy < 0 else slice(0, 2)
-                plan.append(
-                    (dy, dx, fld.at[0:DEEP, src, :, 0:cols], fld.at[0:DEEP, dst, :, 0:cols])
-                )
-                src = slice(RIM, RIM + 1) if dy < 0 else slice(hi - 1, hi)
-                dst = slice(hi, hi + 1) if dy < 0 else slice(1, 2)
-                plan.append(
-                    (dy, dx, fld.at[DEEP:FIELDS, src, :, 0:cols], fld.at[DEEP:FIELDS, dst, :, 0:cols])
-                )
-            else:
-                side = 0 if dx < 0 else 1
-                plan.append((dy, dx, col_send.at[side], col_recv.at[side, centre]))
-        for dy, dx in diagonals:
-            side = 0 if dx < 0 else 1
-            src = slice(0, 2) if dy < 0 else slice(strips - 2, strips)
-            dst = slice(hi, hi + 2) if dy < 0 else slice(0, 2)
-            plan.append((dy, dx, col_send.at[side, src], col_recv.at[side, dst]))
-        copies = []
-        for i, (dy, dx, src, dst) in enumerate(plan):
-            copy = pltpu.make_async_remote_copy(
-                src_ref=src, dst_ref=dst, send_sem=send_sem.at[i], recv_sem=recv_sem.at[i],
-                device_id=(gy + dy, gx + dx), device_id_type=MESH,
-            )
-            copies.append((dy, dx, copy))
-
-            @pl.when(exists(dy, dx))
-            def _():
-                copy.start()
 
         def spread(which, axis):
             buf, ssem, rsem, count = (
@@ -223,33 +271,17 @@
         for copy in scale_x:
             copy.start()
 
-        for copy in scale_x:
-            copy.wait()
-        for n in range(2):
-            sum_y[0, 0, n] = added(0, "gx", n)
-        scale_y = spread(0, "gy")
-        for copy in scale_y:
-            copy.start()
-
-        for dy, dx, copy in copies:
-
-            @pl.when(exists(-dy, -dx))
-            def _():
-                copy.wait_recv()
-
-        def unpack_body(k, _):
-            for tile in range(FIELDS * COLS // 128):
-                nxt = col_recv[0, k, :, tile * 128 : (tile + 1) * 128]
-                prv = col_recv[1, k, :, tile * 128 : (tile + 1) * 128]
-                for i in range(128 // COLS):
-                    a = pltpu.roll(nxt, (-i * COLS) % 128, 1) if i else nxt
-                    move = (128 - COLS - i * COLS) % 128
-                    b = pltpu.roll(prv, move, 1) if move else prv
-                    both = jnp.where(lane < COLS, a, jnp.where(lane >= 128 - COLS, b, 0.0))
-                    fld[tile * (128 // COLS) + i, k, :, cols:width] = both
-            return 0
-
-        lax.fori_loop(0, total, unpack_body, 0)
+        arrived(near)
+        unpack(0)
+        for up in range(2):
+            at, row = (hi + 1, 0) if up else (0, 6)
+            for strip in range(2):
+                packed = row_recv[up, strip]
+                for i in range(min(4, DEEP - 4 * strip)):
+                    move = (row - 2 * i) % 8
+                    x = pltpu.roll(packed, move, 0) if move else packed
+                    inside = jnp.logical_and(sub_own >= row, sub_own < row + 2)
+                    fld[4 * strip + i, at, :, 0:cols] = jnp.where(inside, x, 0.0)
 
         def east(x):
             return pltpu.roll(x, width - 1, 1)
@@ -275,22 +307,26 @@
             gr = jnp.where(mask == 2.0, 1.0, 0.0)
             cce = 0.5 * cov * east(cov)
             ccs = 0.5 * cov * south(cov, cov_n)
-            flags = fld[FLAGS, k]
-            ds = jnp.where(flags >= 2.0, 1.0, 0.0)
             s["cov"][k] = cov
             s["gr"][k] = gr
             s["fri"][k] = fld[BETA, k] * gr
             s["cce"][k] = cce
             s["ccs"][k] = ccs
+            h = fld[H1, k]
+            s["1ce"][k] = cce * (h + east(h))
+            s["1cs"][k] = ccs * (h + south(h, fld[H1, after(k)]))
+            return 0
+
+        lax.fori_loop(0, total, static_body, 0, unroll=2)
+
+        def later_body(k, _):
+            flags, h = fld[FLAGS, k], fld[H0, k]
+            ds = jnp.where(flags >= 2.0, 1.0, 0.0)
             s["ds"][k] = ds
             s["de"][k] = flags - 2.0 * ds
-            for n, h in ((0, H0), (1, H1)):
-                hh = fld[h, k]
-                s[f"{n}ce"][k] = cce * (hh + east(hh))
-                s[f"{n}cs"][k] = ccs * (hh + south(hh, fld[h, after(k)]))
+            s["0ce"][k] = s["cce"][k] * (h + east(h))
+            s["0cs"][k] = s["ccs"][k] * (h + south(h, fld[H0, k + 1]))
             return 0
-
-        lax.fori_loop(0, total, static_body, 0)
 
         H = (H0, H1)
         W = ((U0, V0), (U1, V1))
@@ -335,11 +371,21 @@
                     t[name][k] = value
                 return fsu, fsv, cs
 
-            lax.fori_loop(lo, end, body, (zero, zero, zero))
+            lax.fori_loop(lo, end, body, (zero, zero, zero), unroll=6 if end - lo == total else 5)
 
         forward(1, 0, 0, total)
         forward(1, 1, first, last)
         forward(1, 2, first, last)
+        for copy in scale_x:
+            copy.wait()
+        for n in range(2):
+            sum_y[0, 0, n] = added(0, "gx", n)
+        scale_y = spread(0, "gy")
+        for copy in scale_y:
+            copy.start()
+        arrived(far)
+        unpack(1)
+        lax.fori_loop(first, last, later_body, 0, unroll=2)
         forward(0, 0, first, last)
         forward(0, 1, first, last)
         forward(0, 2, first, last)
@@ -355,7 +401,7 @@
                 return acc
 
             sum_x[1, 0, n] = 0.5 * lax.fori_loop(
-                RIM, RIM + strips, misfit_body, jnp.zeros((8, 128), jnp.float32)
+                RIM, RIM + strips, misfit_body, jnp.zeros((8, 128), jnp.float32), unroll=2
             )
         misfit_x = spread(1, "gx")
         for copy in misfit_x:
@@ -401,7 +447,7 @@
                 emit(n, 2, 0, k, lu, lv)
                 return vs, hs_there
 
-            lax.fori_loop(first, last, body, (zero, zero))
+            lax.fori_loop(first, last, body, (zero, zero), unroll=5)
 
         def backward(n, j, b, end, g_to=None, f_to=None):
             u_ref, v_ref = velocity(n, j)
@@ -445,7 +491,7 @@
                 emit(n, j - 1, 1 - b, k, lu, lv)
                 return xsu, xsv
 
-            lax.fori_loop(first, end, body, (zero,) if finish else (zero, zero))
+            lax.fori_loop(first, end, body, (zero,) if finish else (zero, zero), unroll=5)
 
         transport(1, fld.at[ADJ])
         backward(1, 2, 0, last)
@@ -463,7 +509,7 @@
         transport(0, s["g1"])
         backward(0, 2, 0, last)
         backward(0, 1, 1, last)
-        backward(0, 0, 0, last - 1, s["g0"], s["f0"])
+        backward(0, 0, 0, last, s["g0"], s["f0"])
 
         f_sum = s["f1"][centre, :, 0:cols] + s["f0"][centre, :, 0:cols]
         beta_out[...] = s["gr"][centre, :, 0:cols] * f_sum
@@ -473,7 +519,7 @@
             copy.wait()
         parts = [whole(added(1, "gy", n)) * (1.0 / cell_count) / scales[n] for n in range(2)]
         misfit_out[...] = parts[1] + parts[0]
-        for dy, dx, copy in copies:
+        for dy, dx, copy in near + far:
 
             @pl.when(exists(dy, dx))
             def _():
@@ -501,11 +547,13 @@
         out_specs=(vmem, vmem, vmem),
         scratch_shapes=[
             pltpu.VMEM((FIELDS, total, 8, width), jnp.float32),
-            pltpu.VMEM((2, strips, 8, FIELDS * COLS), jnp.float32),
-            pltpu.VMEM((2, total, 8, FIELDS * COLS), jnp.float32),
+            pltpu.VMEM((FIELDS * COLS // 128, 2, strips, 8, 128), jnp.float32),
+            pltpu.VMEM((FIELDS * COLS // 128, 2, total, 8, 128), jnp.float32),
+            pltpu.VMEM((2, 2, 8, cols), jnp.float32),
+            pltpu.VMEM((2, 2, 8, cols), jnp.float32),
             pltpu.VMEM((2, nx, 2, 8, 128), jnp.float32),
             pltpu.VMEM((2, ny, 2, 8, 128), jnp.float32),
-            dma((10,)), dma((10,)),
+            dma((18,)), dma((18,)),
             dma((2, nx)), dma((2, nx)), dma((2, ny)), dma((2, ny)), dma((len(args),)),
         ]
         + [pltpu.VMEM(arg.shape, arg.dtype) for arg in args]

time: 43.8 us -> 28.4 us (0.65); the launches traced: 43.1 us -> 28.2 us
  Pallas kernels: 38.6 us -> 23.7 us
    pallas_call x1, Pallas kernels: 38.6 us -> 23.7 us  [on_device(): pl.pallas_call(make_kernel(ny, nx, rows, cols, rows * cols * ny * nx), ou...]
where the time goes in v2:
time: 28.4 us; the launch traced here: 28.2 us
  Pallas kernels  23.7 us (83%)
  between operations  2.41 us (8%)
  local copies, waits for them, and re-layouts  2.14 us (8%)
    pallas_call x1, Pallas kernels, on_device(): pl.pallas_call(make_kernel(ny, nx, rows, cols, rows * cols * ny * nx), ou...  23.7 us
    unnamed x4, local copies, waits for them, and re-layouts  2.14 us

profile of v2, /device:TPU:0, one launch (start us, length us, event | category | flops | bytes accessed | tf_op | source)
XLA Modules:
  0.0 28.2 jit_solution(10802528714468639234)
XLA Ops:
  0.6 23.7 %shard_map.103 = (f32[8,8,256]{2,1,0:T(8,128)}, f32[8,8,256]{2,1,0:T(8,128)}, f32[1,1]{1,0:T(1,128)}) custom-call(bf16[2,64,256]{2,1,0:T(8,128)(2,1)} %thick_hbm.1, bf16[2,2,64,256]{3,2,1,0:T(8,128)(2,1)} %vel_hbm.1, bf16[2,64,256]{2,1,0:T(8,128)(2,1)} %slope_hbm.1, f32[64,256]{1,0:T(8,128)} %beta_hbm.1, s32[64,256]{1,0:T(8,128)} %mask_hbm.1, ...), custom_call_target="tpu_custom_call" | custom-call | tf_op jit(solution)/shard_map/pallas_call | solution.py:539
  24.3 0.0 copy-start
  24.3 1.5 %copy.14 = f32[64,256]{1,0:T(8,128)} copy(f32[64,256]{1,0:T(8,128)} %bitcast.4) | data formatting | bytes 131072
  25.8 0.0 copy-done
  25.8 0.6 %copy.15 = f32[64,256]{1,0:T(8,128)} copy(f32[64,256]{1,0:T(8,128)S(1)} %bitcast.3) | data formatting | bytes 131072
Async XLA Ops:
  24.3 1.5 %copy-start = (f32[8,8,256]{2,1,0:T(8,128)S(1)}, f32[8,8,256]{2,1,0:T(8,128)}, u32[]{:S(2)}) copy-start(f32[8,8,256]{2,1,0:T(8,128)} %get-tuple-element.7) | copy-start | bytes 196612

commit v3 on v2

--- a/solution.py
+++ b/solution.py
@@ -130,12 +130,6 @@
                     packed = jnp.where(inside, x, packed)
                 row_send[up, strip] = packed
 
-        beside = [
-            jnp.where(at > 0, 1, 0) + jnp.where(at < count - 1, 1, 0)
-            for at, count in ((gy, ny), (gx, nx))
-        ]
-        pl.semaphore_wait(barrier, (nx - 1) + (ny - 1) + beside[0] * beside[1])
-
         def begin(plan, base):
             copies = []
             for i, (dy, dx, src, dst) in enumerate(plan):
@@ -204,40 +198,6 @@
                 return 0
 
             lax.fori_loop(0, total, unpack_body, 0, unroll=2)
-
-        near = begin(
-            row_plan(slice(0, DEEP))
-            + [(-1, 0, row_send.at[1], row_recv.at[1]), (1, 0, row_send.at[0], row_recv.at[0])],
-            0,
-        )
-        for load in loads[5:]:
-            load.wait()
-        place(FLAGS, flags_in[...])
-        pack(0)
-        near += begin(col_plan(0), 4)
-        place(H0, thick_in[0])
-        place(U0, vel_in[0, 0])
-        place(V0, vel_in[0, 1])
-        place(OU0, obs_in[0, 0])
-        place(OV0, obs_in[0, 1])
-        place(OU1, obs_in[1, 0])
-        place(OV1, obs_in[1, 1])
-        place(ADJ, adj_in[...])
-        far = begin(row_plan(slice(DEEP, FIELDS)), 10)
-        pack(1)
-        far += begin(col_plan(1), 12)
-
-        for n, (ou, ov) in enumerate(((OU0, OV0), (OU1, OV1))):
-            def scale_body(k, acc, ou=ou, ov=ov):
-                a, b = fld[ou, k, :, 0:cols], fld[ov, k, :, 0:cols]
-                t = jnp.where(fld[MASK, k, :, 0:cols] == 2.0, a * a + b * b, 0.0)
-                for c in range(0, cols, 128):
-                    acc = acc + t[:, c : c + 128]
-                return acc
-
-            sum_x[0, 0, n] = lax.fori_loop(
-                RIM, RIM + strips, scale_body, jnp.zeros((8, 128), jnp.float32), unroll=2
-            )
 
         def spread(which, axis):
             buf, ssem, rsem, count = (
@@ -267,9 +227,49 @@
         def whole(tile):
             return jnp.sum(jnp.sum(tile, axis=1, keepdims=True), axis=0, keepdims=True)
 
+        for load in loads[5:]:
+            load.wait()
+        place(FLAGS, flags_in[...])
+        place(H0, thick_in[0])
+        place(U0, vel_in[0, 0])
+        place(V0, vel_in[0, 1])
+        place(OU0, obs_in[0, 0])
+        place(OV0, obs_in[0, 1])
+        place(OU1, obs_in[1, 0])
+        place(OV1, obs_in[1, 1])
+        place(ADJ, adj_in[...])
+        pack(0)
+        for n, (ou, ov) in enumerate(((OU0, OV0), (OU1, OV1))):
+            def scale_body(k, acc, ou=ou, ov=ov):
+                a, b = fld[ou, k, :, 0:cols], fld[ov, k, :, 0:cols]
+                t = jnp.where(fld[MASK, k, :, 0:cols] == 2.0, a * a + b * b, 0.0)
+                for c in range(0, cols, 128):
+                    acc = acc + t[:, c : c + 128]
+                return acc
+
+            sum_x[0, 0, n] = lax.fori_loop(
+                RIM, RIM + strips, scale_body, jnp.zeros((8, 128), jnp.float32), unroll=2
+            )
+
+        pack(1)
+        beside = [
+            jnp.where(at > 0, 1, 0) + jnp.where(at < count - 1, 1, 0)
+            for at, count in ((gy, ny), (gx, nx))
+        ]
+        pl.semaphore_wait(barrier, (nx - 1) + (ny - 1) + beside[0] * beside[1])
+
+        near = begin(
+            row_plan(slice(0, DEEP))
+            + [(-1, 0, row_send.at[1], row_recv.at[1]), (1, 0, row_send.at[0], row_recv.at[0])],
+            0,
+        )
+        near += begin(col_plan(0), 4)
         scale_x = spread(0, "gx")
         for copy in scale_x:
             copy.start()
+
+        far = begin(row_plan(slice(DEEP, FIELDS)), 10)
+        far += begin(col_plan(1), 12)
 
         arrived(near)
         unpack(0)
@@ -282,6 +282,14 @@
                     x = pltpu.roll(packed, move, 0) if move else packed
                     inside = jnp.logical_and(sub_own >= row, sub_own < row + 2)
                     fld[4 * strip + i, at, :, 0:cols] = jnp.where(inside, x, 0.0)
+
+        for copy in scale_x:
+            copy.wait()
+        for n in range(2):
+            sum_y[0, 0, n] = added(0, "gx", n)
+        scale_y = spread(0, "gy")
+        for copy in scale_y:
+            copy.start()
 
         def east(x):
             return pltpu.roll(x, width - 1, 1)
@@ -376,13 +384,6 @@
         forward(1, 0, 0, total)
         forward(1, 1, first, last)
         forward(1, 2, first, last)
-        for copy in scale_x:
-            copy.wait()
-        for n in range(2):
-            sum_y[0, 0, n] = added(0, "gx", n)
-        scale_y = spread(0, "gy")
-        for copy in scale_y:
-            copy.start()
         arrived(far)
         unpack(1)
         lax.fori_loop(first, last, later_body, 0, unroll=2)
@@ -539,8 +540,8 @@
     beta, thick, misfit = pl.pallas_call(
         make_kernel(ny, nx, rows, cols, rows * cols * ny * nx),
         out_shape=(
-            jax.ShapeDtypeStruct((strips, 8, cols), jnp.float32),
-            jax.ShapeDtypeStruct((strips, 8, cols), jnp.float32),
+            pltpu.VMEM((strips, 8, cols), jnp.float32),
+            pltpu.VMEM((strips, 8, cols), jnp.float32),
             jax.ShapeDtypeStruct((1, 1), jnp.float32),
         ),
         in_specs=[pl.BlockSpec(memory_space=pltpu.HBM)] * len(args),

time: 28.4 us -> 27.4 us (0.965)
  local copies, waits for them, and re-layouts: 2.14 us -> 1.26 us
    unnamed x4 -> x2, local copies, waits for them, and re-layouts: 2.14 us -> 1.26 us
where the time goes in v3:
time: 27.4 us; the launch traced here: 27.2 us
  Pallas kernels  23.6 us (86%)
  between operations  2.33 us (9%)
  local copies, waits for them, and re-layouts  1.26 us (5%)
    pallas_call x1, Pallas kernels, on_device(): pl.pallas_call(make_kernel(ny, nx, rows, cols, rows * cols * ny * nx), ou...  23.6 us
    unnamed x2, local copies, waits for them, and re-layouts  1.26 us

profile of v3, /device:TPU:0, one launch (start us, length us, event | category | flops | bytes accessed | tf_op | source)
XLA Modules:
  0.0 27.2 jit_solution(4130795055774943788)
XLA Ops:
  0.6 23.6 %shard_map.103 = (f32[8,8,256]{2,1,0:T(8,128)S(1)}, f32[8,8,256]{2,1,0:T(8,128)S(1)}, f32[1,1]{1,0:T(1,128)}) custom-call(bf16[2,64,256]{2,1,0:T(8,128)(2,1)} %thick_hbm.1, bf16[2,2,64,256]{3,2,1,0:T(8,128)(2,1)} %vel_hbm.1, bf16[2,64,256]{2,1,0:T(8,128)(2,1)} %slope_hbm.1, f32[64,256]{1,0:T(8,128)} %beta_hbm.1, s32[64,256]{1,0:T(8,128)} %mask_hbm.1, ...), custom_call_target="tpu_custom_call" | custom-call | tf_op jit(solution)/shard_map/pallas_call | solution.py:540
  24.3 0.6 %copy.14 = f32[64,256]{1,0:T(8,128)} copy(f32[64,256]{1,0:T(8,128)S(1)} %bitcast.4) | data formatting | bytes 131072
  24.9 0.6 %copy.15 = f32[64,256]{1,0:T(8,128)} copy(f32[64,256]{1,0:T(8,128)S(1)} %bitcast.3) | data formatting | bytes 131072

commit v4 on v3

--- a/solution.py
+++ b/solution.py
@@ -184,7 +184,7 @@
                     col_send[tile, side, k] = packed
                 return 0
 
-            lax.fori_loop(0, strips, pack_body, 0, unroll=2)
+            lax.fori_loop(0, strips, pack_body, 0, unroll=4)
 
         def unpack(tile):
             def unpack_body(k, _):
@@ -197,7 +197,7 @@
                     fld[tile * per_tile + i, k, :, cols:width] = both
                 return 0
 
-            lax.fori_loop(0, total, unpack_body, 0, unroll=2)
+            lax.fori_loop(0, total, unpack_body, 0, unroll=4)
 
         def spread(which, axis):
             buf, ssem, rsem, count = (
@@ -248,7 +248,7 @@
                 return acc
 
             sum_x[0, 0, n] = lax.fori_loop(
-                RIM, RIM + strips, scale_body, jnp.zeros((8, 128), jnp.float32), unroll=2
+                RIM, RIM + strips, scale_body, jnp.zeros((8, 128), jnp.float32), unroll=4
             )
 
         pack(1)
@@ -284,7 +284,7 @@
                     fld[4 * strip + i, at, :, 0:cols] = jnp.where(inside, x, 0.0)
 
         for copy in scale_x:
-            copy.wait()
+            copy.wait_recv()
         for n in range(2):
             sum_y[0, 0, n] = added(0, "gx", n)
         scale_y = spread(0, "gy")
@@ -325,7 +325,7 @@
             s["1cs"][k] = ccs * (h + south(h, fld[H1, after(k)]))
             return 0
 
-        lax.fori_loop(0, total, static_body, 0, unroll=2)
+        lax.fori_loop(0, total, static_body, 0, unroll=4)
 
         def later_body(k, _):
             flags, h = fld[FLAGS, k], fld[H0, k]
@@ -386,7 +386,7 @@
         forward(1, 2, first, last)
         arrived(far)
         unpack(1)
-        lax.fori_loop(first, last, later_body, 0, unroll=2)
+        lax.fori_loop(first, last, later_body, 0, unroll=5)
         forward(0, 0, first, last)
         forward(0, 1, first, last)
         forward(0, 2, first, last)
@@ -402,14 +402,14 @@
                 return acc
 
             sum_x[1, 0, n] = 0.5 * lax.fori_loop(
-                RIM, RIM + strips, misfit_body, jnp.zeros((8, 128), jnp.float32), unroll=2
+                RIM, RIM + strips, misfit_body, jnp.zeros((8, 128), jnp.float32), unroll=4
             )
         misfit_x = spread(1, "gx")
         for copy in misfit_x:
             copy.start()
 
         for copy in scale_y:
-            copy.wait()
+            copy.wait_recv()
         scales = [whole(added(0, "gy", n)) * (1.0 / cell_count) + EPSILON for n in range(2)]
 
         def emit(n, j, b, k, lu, lv):
@@ -500,7 +500,7 @@
         backward(1, 0, 0, last, s["g1"], s["f1"])
 
         for copy in misfit_x:
-            copy.wait()
+            copy.wait_recv()
         for n in range(2):
             sum_y[1, 0, n] = added(1, "gx", n)
         misfit_y = spread(1, "gy")
@@ -517,7 +517,7 @@
         thick_out[...] = s["g0"][centre, :, 0:cols]
 
         for copy in misfit_y:
-            copy.wait()
+            copy.wait_recv()
         parts = [whole(added(1, "gy", n)) * (1.0 / cell_count) / scales[n] for n in range(2)]
         misfit_out[...] = parts[1] + parts[0]
         for dy, dx, copy in near + far:
@@ -525,6 +525,8 @@
             @pl.when(exists(dy, dx))
             def _():
                 copy.wait_send()
+        for copy in scale_x + scale_y + misfit_x + misfit_y:
+            copy.wait_send()
 
     return kernel
 

time: 27.4 us -> 26.5 us (0.967)
  Pallas kernels: 23.6 us -> 22.7 us
    pallas_call x1, Pallas kernels: 23.6 us -> 22.7 us  [on_device(): pl.pallas_call(make_kernel(ny, nx, rows, cols, rows * cols * ny * nx), ou...]
where the time goes in v4:
time: 26.5 us; the launch traced here: 26.3 us
  Pallas kernels  22.7 us (86%)
  between operations  2.33 us (9%)
  local copies, waits for them, and re-layouts  1.26 us (5%)
    pallas_call x1, Pallas kernels, on_device(): pl.pallas_call(make_kernel(ny, nx, rows, cols, rows * cols * ny * nx), ou...  22.7 us
    unnamed x2, local copies, waits for them, and re-layouts  1.26 us

profile of v4, /device:TPU:0, one launch (start us, length us, event | category | flops | bytes accessed | tf_op | source)
XLA Modules:
  0.0 26.3 jit_solution(6562431206018143800)
XLA Ops:
  0.6 22.7 %shard_map.103 = (f32[8,8,256]{2,1,0:T(8,128)S(1)}, f32[8,8,256]{2,1,0:T(8,128)S(1)}, f32[1,1]{1,0:T(1,128)}) custom-call(bf16[2,64,256]{2,1,0:T(8,128)(2,1)} %thick_hbm.1, bf16[2,2,64,256]{3,2,1,0:T(8,128)(2,1)} %vel_hbm.1, bf16[2,64,256]{2,1,0:T(8,128)(2,1)} %slope_hbm.1, f32[64,256]{1,0:T(8,128)} %beta_hbm.1, s32[64,256]{1,0:T(8,128)} %mask_hbm.1, ...), custom_call_target="tpu_custom_call" | custom-call | tf_op jit(solution)/shard_map/pallas_call | solution.py:542
  23.3 0.6 %copy.14 = f32[64,256]{1,0:T(8,128)} copy(f32[64,256]{1,0:T(8,128)S(1)} %bitcast.4) | data formatting | bytes 131072
  24.0 0.6 %copy.15 = f32[64,256]{1,0:T(8,128)} copy(f32[64,256]{1,0:T(8,128)S(1)} %bitcast.3) | data formatting | bytes 131072
